TPU v7x, 32 devices: a whole 2x2x4 slice. The times are simulated.
32 devices in a mesh: dp: 8 (over y, x, core), tensor: 4 (over z).
Axes of the slice: x: 2, y: 2, z: 4, core: 2. Of those that a mesh axis runs over, the one named last changes fastest.
Arguments:
- activations: bfloat16 [160, 6656], P('dp', 'tensor'), may hold values from -6 to 6
- weight_codes: int32 [6656, 8192], P(('tensor', 'dp')), may hold values from 0 to 15
- scale_index: int32 [6656, 64], P(('tensor', 'dp')), may hold values from 0 to 15, as said below
- scale_table: float32 [16], replicated
- bit_widths: int32 [1, 6656, 64], P(None, ('tensor', 'dp')), may hold values from 2 to 4
Outputs:
- base_output: bfloat16 [160, 8192], P('tensor', 'dp')
- scores: float32 [1, 160], P(None, 'tensor')
Inputs may be any that keep to these rules, and one draw needn't show every extreme that they name: `scale_index`: an entry of scale_table for each row and each group of 128 columns.
All inputs are finite; a program needn't handle non-finite values.
Results may differ from a plain program's by a relative error of at most 0.0058.
Values may be sent and summed in bfloat16 or wider, within the bound.
A program may use at most 128 MiB of HBM per device.

v0:
```python
import math

import jax
import jax.numpy as jnp
from jax import lax
from jax.sharding import PartitionSpec as P

HB = 128
NCAND = 1


score_divisor = 512.0


def swapped(block, axis, bit):
    count = lax.axis_size(axis)
    route = []
    for low in range(count):
        high = low | 1 << bit
        if high != low and high < count:
            route += [(low, high), (high, low)]
    return lax.ppermute(block, axis, route)


def sylvester(order_size):
    positions = jnp.arange(order_size, dtype=jnp.int32)
    intersection = positions[:, None] & positions[None, :]
    parity = jnp.zeros((order_size, order_size), jnp.int32)
    for shift_bit in range(max(order_size.bit_length() - 1, 0)):
        parity = parity + (intersection >> shift_bit & 1)
    parity = parity % 2
    return (1 - 2 * parity).astype(jnp.float32)


def dequantize(grouped, index_rows, scale_table, bits_rows):
    one_hot = (index_rows[..., None] == jnp.arange(scale_table.shape[0], dtype=jnp.int32)).astype(
        jnp.float32
    )
    scales = jnp.sum(one_hot * scale_table, axis=-1)
    base_w = ((grouped - 8).astype(jnp.float32) * scales[..., None]).astype(jnp.bfloat16)
    step_size = jnp.where(bits_rows == 2, 4, jnp.where(bits_rows == 3, 2, 1)).astype(jnp.int32)[
        ..., None
    ]
    cand_codes = grouped[None] // step_size * step_size + step_size // 2
    cand_w = ((cand_codes - 8).astype(jnp.float32) * scales[None, :, :, None]).astype(jnp.bfloat16)
    row_count = grouped.shape[0]
    col_count = grouped.shape[1] * grouped.shape[2]
    return jnp.concatenate([base_w[None], cand_w], axis=0).reshape(NCAND + 1, row_count, col_count)


def local(activations, weight_codes, scale_index, scale_table, bit_widths):
    tensor_size = lax.axis_size("tensor")
    tok_rows, feat_width = activations.shape
    block_signs = sylvester(HB).astype(jnp.bfloat16)
    blocked = jnp.einsum(
        "rnb,bc->rnc",
        activations.reshape(tok_rows, feat_width // HB, HB),
        block_signs,
        preferred_element_type=jnp.float32,
    ).reshape(tok_rows, feat_width)
    mixed_rows = blocked
    my_index = lax.axis_index("tensor")
    for section_bit in range(tensor_size.bit_length() - 1):
        partner = swapped(mixed_rows, "tensor", section_bit)
        upper_half = my_index >> section_bit & 1 == 1
        mixed_rows = jnp.where(upper_half, partner - mixed_rows, mixed_rows + partner)
    rotated = (mixed_rows * (1.0 / math.sqrt(HB * tensor_size))).astype(jnp.bfloat16)
    all_tokens = lax.all_gather(rotated, "dp", axis=0, tiled=True)
    store_rows, model_width = weight_codes.shape
    group_count = scale_index.shape[1]
    group_width = model_width // group_count
    code_wire = weight_codes.reshape(store_rows, group_count, group_width).astype(jnp.bfloat16)
    index_wire = scale_index.astype(jnp.bfloat16)
    bits_wire = jnp.transpose(bit_widths, (1, 2, 0)).astype(jnp.bfloat16)
    code_home, index_home, bits_home = (
        lax.all_to_all(code_wire, "dp", split_axis=1, concat_axis=0, tiled=True),
        lax.all_to_all(index_wire, "dp", split_axis=1, concat_axis=0, tiled=True),
        lax.all_to_all(bits_wire, "dp", split_axis=1, concat_axis=0, tiled=True),
    )
    local_grouped = code_home.astype(jnp.int32)
    local_index = index_home.astype(jnp.int32)
    local_bits = jnp.transpose(bits_home.astype(jnp.int32), (2, 0, 1))
    local_weights = dequantize(local_grouped, local_index, scale_table, local_bits)
    token_sums = lax.psum_scatter(
        jnp.einsum("tf,kfd->tkd", all_tokens, local_weights, preferred_element_type=jnp.float32),
        "tensor",
        scatter_dimension=0,
        tiled=True,
    )
    token_sums = jnp.transpose(token_sums, (1, 0, 2))
    base_rows = token_sums[0]
    cand_diffs = token_sums[1:] - base_rows[None]
    block_scores = jnp.sum(cand_diffs * cand_diffs, axis=2) / score_divisor
    scores = lax.psum(block_scores, "dp")
    return (base_rows.astype(jnp.bfloat16), scores)


def solution(mesh):
    in_specs = (
        P("dp", "tensor"),
        P(("tensor", "dp"), None),
        P(("tensor", "dp"), None),
        P(),
        P(None, ("tensor", "dp"), None),
    )
    out_specs = (P("tensor", "dp"), P(None, "tensor"))
    return jax.shard_map(local, mesh=mesh, in_specs=in_specs, out_specs=out_specs, check_vma=False)
```

profile of v0, /device:TPU:0, one launch (start us, length us, event | category | flops | bytes accessed | tf_op | source)
XLA Modules:
  0.0 266.4 jit_solution(17072399943461936469)
XLA Ops:
  8.6 5.2 %all-to-all-start.1 = ((bf16[208,8,8]{0,2,1:T(8,128)(2,1)}), bf16[208,8,8]{0,2,1:T(8,128)(2,1)S(1)}, u32[]{:S(2)}, u32[]{:S(2)}) async-start(bf16[208,8,8]{0,2,1:T(8,128)(2,1)} %convert_bitcast_fusion.4), calls=%async_computation.1 | async-start | bytes 65536 | tf_op jit(solution)/shard_map/all_to_all | solution.py:77
  16.8 1.9 all-to-all-done.1
  18.6 3.3 %all-to-all-start.2 = ((bf16[8,2,832]{2,1,0:T(2,128)(2,1)}), bf16[8,2,832]{2,1,0:T(2,128)(2,1)S(1)}, u32[]{:S(2)}, u32[]{:S(2)}) async-start(bf16[8,2,832]{2,1,0:T(2,128)(2,1)} %reshape.332), calls=%async_computation.2 | async-start | bytes 57344 | tf_op jit(solution)/shard_map/all_to_all | solution.py:78
  22.0 5.2 %copy_bitcast_fusion = bf16[208,64,128]{2,0,1:T(8,128)(2,1)} fusion(s32[208,8192]{1,0:T(8,128)} %param.6), kind=kLoop, calls=%fused_computation.16 | loop fusion | flops 1703936 | bytes 10223616 | tf_op jit(solution)/shard_map/convert_element_type | solution.py:72
  27.2 4.1 %all-to-all-start = ((bf16[208,64,128]{2,0,1:T(8,128)(2,1)}), bf16[208,64,128]{2,0,1:T(8,128)(2,1)S(1)}, u32[]{:S(2)}, u32[]{:S(2)}) async-start(bf16[208,64,128]{2,0,1:T(8,128)(2,1)} %copy_bitcast_fusion), calls=%async_computation | async-start | bytes 6815744 | tf_op jit(solution)/shard_map/all_to_all | solution.py:76
  40.2 2.0 copy.48
  42.2 1.7 add_select_fusion.1
  43.9 2.6 collective-permute-start.1
  50.0 8.1 %add.97 = s32[1664,8,128]{2,1,0:T(8,128)} broadcast(s32[1664,8]{1,0:T(8,128)} %copy.50), dimensions={0,1} | broadcast | bytes 6868992 | tf_op jit(solution)/shard_map/add | solution.py:44
  58.0 8.1 %add.98 = s32[1,1664,1024]{2,1,0:T(8,128)} reshape(s32[1664,8,128]{2,1,0:T(8,128)} %add.97) | data formatting | bytes 13631488 | tf_op jit(solution)/shard_map/add | solution.py:44
  66.1 5.3 %mul.73 = f32[1664,8,128]{2,1,0:T(8,128)} broadcast(f32[1664,8]{1,0:T(8,128)} %copy.45), dimensions={0,1} | broadcast | bytes 6868992 | tf_op jit(solution)/shard_map/mul | solution.py:40
  71.4 8.2 %mul.74 = f32[1,1664,1024]{2,1,0:T(8,128)} reshape(f32[1664,8,128]{2,1,0:T(8,128)} %mul.73) | data formatting | bytes 13631488 | tf_op jit(solution)/shard_map/mul | solution.py:40
  79.6 8.0 %rem.51 = s32[1664,8,128]{2,1,0:T(8,128)} broadcast(s32[1664,8]{1,0:T(8,128)} %copy.49), dimensions={0,1} | broadcast | bytes 6868992 | tf_op jit(solution)/shard_map/jit(floor_divide)/rem | solution.py:44
  87.6 8.1 %rem.52 = s32[1,1664,1024]{2,1,0:T(8,128)} reshape(s32[1664,8,128]{2,1,0:T(8,128)} %rem.51) | data formatting | bytes 13631488 | tf_op jit(solution)/shard_map/jit(floor_divide)/rem | solution.py:44
  95.7 8.0 %ne.73 = s32[1664,8,128]{2,1,0:T(8,128)} broadcast(s32[1664,8]{1,0:T(8,128)} %copy.48), dimensions={0,1} | broadcast | bytes 6868992 | tf_op jit(solution)/shard_map/jit(floor_divide)/ne | solution.py:44
  103.7 8.1 %ne.74 = s32[1,1664,1024]{2,1,0:T(8,128)} reshape(s32[1664,8,128]{2,1,0:T(8,128)} %ne.73) | data formatting | bytes 13631488 | tf_op jit(solution)/shard_map/jit(floor_divide)/ne | solution.py:44
  112.8 11.6 %all-gather = bf16[8,20,1664]{2,1,0:T(8,128)(2,1)} all-gather(bf16[1,20,1664]{2,1,0:T(8,128)(2,1)S(1)} %fusion.14), channel_id=1, replica_groups=mesh['dp'=8,'tensor'=4] {'dp'}, dimensions={0}, use_global_device_ids=true | all-gather | bytes 599040 | tf_op jit(solution)/shard_map/all_gather | solution.py:68
  124.5 2.0 reshape.330
  127.5 3.2 %copy.43 = s32[8,208,8,128]{3,2,1,0:T(8,128)} copy(s32[8,208,8,128]{3,2,0,1:T(8,128)S(1)} %convert_bitcast_fusion) | data formatting | bytes 13631488 | tf_op jit(solution)/shard_map/convert_element_type | solution.py:80
  130.8 8.1 %reshape.319 = s32[1,1664,1024]{2,1,0:T(8,128)} reshape(s32[8,208,8,128]{3,2,1,0:T(8,128)} %copy.43) | data formatting | bytes 13631488 | tf_op jit(solution)/shard_map/convert_element_type | solution.py:80
  138.9 72.8 %multiply_convert_fusion = (bf16[1,1664,1024]{2,1,0:T(8,128)(2,1)S(1)}, bf16[1,1664,1024]{2,1,0:T(8,128)(2,1)S(1)}) fusion(f32[1,1664,1024]{2,1,0:T(8,128)} %mul.74, s32[1,1664,1024]{2,1,0:T(8,128)} %reshape.319, s32[1,1664,1024]{2,1,0:T(8,128)} %add.98, s32[1,1664,1024]{2,1,0:T(8,128)} %rem.52, s32[1,1664,1024]{2,1,0:T(8,128)} %ne.74), kind=kLoop, calls=%fused_computation.14 | loop fusion | flops 30670848 | bytes 40894464 | tf_op jit(solution)/shard_map/convert_element_type | solution.py:40
  211.7 2.5 fusion.6
  214.2 28.8 %reduce-scatter.2.cloned.1.call-done = f32[40,2,1024]{2,0,1:T(8,128)} async-done(((f32[160,2,1024]{2,0,1:T(8,128)}), f32[40,2,1024]{2,0,1:T(8,128)}) %reduce-scatter.2.cloned.1.call-update) | async-done | bytes 327696 | tf_op jit(solution)/shard_map/reduce_scatter | solution.py:84
  245.6 13.9 %psum.7 = f32[1,40]{1,0:T(1,128)} all-reduce(f32[1,40]{1,0:T(1,128)S(1)} %multiply_bitcast_fusion), channel_id=1, replica_groups=mesh['dp'=8,'tensor'=4] {'dp'}, use_global_device_ids=true, to_apply=%region_3.4 | all-reduce | flops 40 | bytes 320 | tf_op jit(solution)/shard_map/psum | solution.py:94
  (41 shorter events, 21.6 us)
Async XLA Ops:
  8.6 10.0 %all-to-all-start.1 = ((bf16[208,8,8]{0,2,1:T(8,128)(2,1)}), bf16[208,8,8]{0,2,1:T(8,128)(2,1)S(1)}, u32[]{:S(2)}, u32[]{:S(2)}) async-start(bf16[208,8,8]{0,2,1:T(8,128)(2,1)} %convert_bitcast_fusion.4), calls=%async_computation.1 | async-start | bytes 65536 | tf_op jit(solution)/shard_map/all_to_all | solution.py:77
  18.6 8.5 %copy-start.1 = (bf16[208,8,8]{0,2,1:T(8,128)(2,1)}, bf16[208,8,8]{0,2,1:T(8,128)(2,1)S(1)}, u32[]{:S(2)}) copy-start(bf16[208,8,8]{0,2,1:T(8,128)(2,1)S(1)} %all-to-all-done.1) | copy-start | bytes 79876
  18.6 8.5 %all-to-all-start.2 = ((bf16[8,2,832]{2,1,0:T(2,128)(2,1)}), bf16[8,2,832]{2,1,0:T(2,128)(2,1)S(1)}, u32[]{:S(2)}, u32[]{:S(2)}) async-start(bf16[8,2,832]{2,1,0:T(2,128)(2,1)} %reshape.332), calls=%async_computation.2 | async-start | bytes 57344 | tf_op jit(solution)/shard_map/all_to_all | solution.py:78
  27.1 19.3 %copy-start.2 = (f32[16]{0:T(128)S(1)}, f32[16]{0:T(128)}, u32[]{:S(2)}) copy-start(f32[16]{0:T(128)} %param.8) | copy-start | bytes 196
  27.2 99.3 %all-to-all-start = ((bf16[208,64,128]{2,0,1:T(8,128)(2,1)}), bf16[208,64,128]{2,0,1:T(8,128)(2,1)S(1)}, u32[]{:S(2)}, u32[]{:S(2)}) async-start(bf16[208,64,128]{2,0,1:T(8,128)(2,1)} %copy_bitcast_fusion), calls=%async_computation | async-start | bytes 6815744 | tf_op jit(solution)/shard_map/all_to_all | solution.py:76
  31.3 211.6 %reduce-scatter.2.cloned.1.call-start = ((), (), s32[]{:S(2)}) async-start(), calls=%async_computation.4 | async-start | bytes 1638400 | tf_op jit(solution)/shard_map/reduce_scatter | solution.py:84
  34.9 7.3 %collective-permute-start = (f32[20,1664]{1,0:T(8,128)}, f32[20,1664]{1,0:T(8,128)}, u32[]{:S(2)}, u32[]{:S(2)}) collective-permute-start(f32[20,1664]{1,0:T(8,128)} %bitcast.18), channel_id=1, source_target_pairs={{0,1},{1,0},{2,3},{3,2},{4,5},{5,4},{6,7},{7,6},{8,9},{9,8},{10,11... | collective-permute-start | bytes 399368 | tf_op jit(solution)/shard_map/ppermute | solution.py:22
  43.9 68.0 %collective-permute-start.1 = (f32[20,1664]{1,0:T(8,128)}, f32[20,1664]{1,0:T(8,128)}, u32[]{:S(2)}, u32[]{:S(2)}) collective-permute-start(f32[20,1664]{1,0:T(8,128)} %add_select_fusion.1), channel_id=1, source_target_pairs={{0,2},{2,0},{1,3},{3,1},{4,6},{6,4},{5,7},{7,5},{8,10},{10,8},{9,1... | collective-permute-start | bytes 399368 | tf_op jit(solution)/shard_map/ppermute | solution.py:22
  138.9 72.8 %copy-start = (bf16[160,1664,1]{1,0,2:T(8,128)(2,1)S(1)}, bf16[160,1664,1]{1,0,2:T(8,128)(2,1)}, u32[]{:S(2)}) copy-start(bf16[160,1664,1]{1,0,2:T(8,128)(2,1)} %reshape.330) | copy-start | bytes 1597444
Sparse Core Ops, SparseCore 0:
  214.3 28.6 reduce-scatter.1
where the time goes:
time: 269 us; the launch traced here: 266 us
  other arithmetic  88.6 us (33%)
  local copies, waits for them, and re-layouts  87.1 us (32%)
  waiting for transfers between devices  30.7 us (11%)
  blocking collectives  25.5 us (9%)
  starting transfers between devices  16.9 us (6%)
  between operations  14.1 us (5%)
  matrix products  3.59 us (1%)
    convert_element_type x1, other arithmetic, dequantize(): ((grouped - 8).astype(jnp.float32) * scales[..., None]).astype(jnp.bfloat16)  72.8 us
    reduce_scatter x1, waiting for transfers between devices, local(): lax.psum_scatter(jnp.einsum('tf,kfd->tkd', all_tokens, local_weights, pre...  28.8 us
    add x2, local copies, waits for them, and re-layouts, dequantize(): cand_codes = grouped[None] // step_size * step_size + step_size // 2  16.2 us
    ne x2, local copies, waits for them, and re-layouts, dequantize(): cand_codes = grouped[None] // step_size * step_size + step_size // 2  16.1 us
    rem x2, local copies, waits for them, and re-layouts, dequantize(): cand_codes = grouped[None] // step_size * step_size + step_size // 2  16.1 us
    psum x1, blocking collectives, local(): scores = lax.psum(block_scores, 'dp')  13.9 us
    mul x2, local copies, waits for them, and re-layouts, dequantize(): (grouped - 8).astype(jnp.float32) * scales[..., None]  13.5 us
    all_gather x1, blocking collectives, local(): all_tokens = lax.all_gather(rotated, 'dp', axis=0, tiled=True)  11.6 us
  transfers between devices with their start and end apart: 6, of which 2 were waited for; matrix products, arithmetic and copies ran while one was open for 33% of the time, Pallas kernels for 0%

commit v1 on v0

v1 whole, which is shorter than its diff:
```python
import functools
import math

import jax
import jax.numpy as jnp
import numpy as np
from jax import lax
from jax.experimental import pallas as pl
from jax.experimental.pallas import tpu as pltpu
from jax.sharding import PartitionSpec as P

HB = 128
SCORE_DIVISOR = 512.0
MESH = pl.DeviceIdType.MESH
BF16, F32, I32 = jnp.bfloat16, jnp.float32, jnp.int32


def sylvester(order):
    bits = np.arange(order)[:, None] & np.arange(order)[None, :]
    parity = np.zeros((order, order), np.int32)
    for shift in range(order.bit_length()):
        parity += (bits >> shift) & 1
    return (1 - 2 * (parity % 2)).astype(np.float32)


def up16(count):
    return -(-count // 16) * 16


def sizes(ndp, nt, act_shape, code_shape):
    tl, width = act_shape
    rows, model = code_shape
    z = dict(ndp=ndp, nt=nt, chips=ndp // 2, tl=tl, tp=up16(tl), nblk=width // HB, rows=rows)
    z["rp"] = up16(rows)
    z["cols"] = model // ndp
    z["tokens"] = tl * ndp
    z["tt"] = z["tokens"] // nt
    pair = 2 * rows
    spans = [(c * pair + pair - 1) // HB - c * pair // HB + 1 for c in range(z["chips"])]
    z["nb"] = min(max(spans), z["nblk"])
    z["cw"] = 256 if z["cols"] % 256 == 0 else z["cols"]
    z["nch"] = z["cols"] // z["cw"]
    return z


def window_start(z, chip):
    return jnp.minimum(chip * (2 * z["rows"]) // HB, z["nblk"] - z["nb"])


def kernel(z, act_ref, code_hbm, index_ref, table_ref, bits_ref, had_ref, out_ref, score_ref,
           codes, xs, rot, win, wpad, lhs, weights, wrecv, psend, prec, acc, zsend, zrec, srec,
           code_sem, xs_s, xs_r, win_s, win_r, w_s, w_r, p_s, p_r, z_s, z_r, s_s, s_r):
    ndp, nt, chips = z["ndp"], z["nt"], z["chips"]
    tl, tp, nblk, nb = z["tl"], z["tp"], z["nblk"], z["nb"]
    rows, rp, cols, tokens, tt = z["rows"], z["rp"], z["cols"], z["tokens"], z["tt"]
    cw, nch = z["cw"], z["nch"]
    d = lax.axis_index("dp")
    s = lax.axis_index("tensor")
    chip, core = d // 2, d % 2

    loads = []
    for q in range(chips):
        span = pl.ds(q * 2 * cols, 2 * cols)
        load = pltpu.make_async_copy(code_hbm.at[:, span], codes.at[:, span], code_sem.at[q])
        load.start()
        loads.append(load)

    barrier = pltpu.get_barrier_semaphore()
    for k in range(1, ndp):
        pl.semaphore_signal(barrier, inc=1, device_id=(lax.rem(d + k, ndp), s), device_id_type=MESH)
    for k in range(1, nt):
        pl.semaphore_signal(barrier, inc=1, device_id=(d, lax.rem(s + k, nt)), device_id_type=MESH)

    xs[0] = jnp.zeros(xs.shape[1:], BF16)
    for n in range(nblk):
        xs[0, n * tp:n * tp + tl, :] = act_ref[:, n * HB:(n + 1) * HB]

    pl.semaphore_wait(barrier, ndp - 1 + nt - 1)

    xcopies = []
    for k in range(1, nt):
        copy = pltpu.make_async_remote_copy(
            src_ref=xs.at[0], dst_ref=xs.at[k], send_sem=xs_s.at[k], recv_sem=xs_r.at[k],
            device_id=(d, lax.rem(s + k, nt)), device_id_type=MESH)
        copy.start()
        xcopies.append(copy)

    index = index_ref[...]
    scales = jnp.zeros(index.shape, F32)
    for i in range(table_ref.shape[0]):
        scales = jnp.where(index == i, table_ref[i], scales)
    bits = bits_ref[...]
    step = jnp.where(bits == 2, 4, jnp.where(bits == 3, 2, 1)).astype(I32)

    if rp != rows:
        weights[...] = jnp.zeros(weights.shape, BF16)
    groups = cols // HB
    wcopies = []

    def dequantize(q):
        rel = lax.rem(q - chip + chips, chips)
        loads[q].wait()
        for half in range(2):
            away = lax.rem(core + half, 2)
            for g in range(groups):
                gg = (q * 2 + half) * groups + g
                c = codes[:, gg * HB:(gg + 1) * HB]
                sc = scales[:, gg:gg + 1]
                st = step[:, gg:gg + 1]
                base = ((c - 8).astype(F32) * sc).astype(BF16)
                cand = (((c & -st) + ((st >> 1) - 8)).astype(F32) * sc).astype(BF16)
                gap = (cand.astype(F32) - base.astype(F32)).astype(BF16)
                weights[away, rel, 0, 0:rows, g * HB:(g + 1) * HB] = base
                weights[away, rel, 1, 0:rows, g * HB:(g + 1) * HB] = gap
        copy = pltpu.make_async_remote_copy(
            src_ref=weights.at[1, rel], dst_ref=wrecv.at[rel], send_sem=w_s.at[q],
            recv_sem=w_r.at[q], device_id=(chip * 2 + 1 - core, s), device_id_type=MESH)
        copy.start()
        wcopies.append(copy)

    def rotate():
        total = jnp.zeros((nblk * tp, HB), F32)
        for k in range(nt):
            if k:
                xcopies[k - 1].wait_recv()
            src = lax.rem(s - k + nt, nt)
            parity = 0
            for b in range(max(nt.bit_length() - 1, 0)):
                parity = parity + (src // 2 ** b % 2) * (s // 2 ** b % 2)
            sign = (1 - 2 * (parity % 2)).astype(F32)
            total = total + sign * jnp.dot(xs[k], had_ref[...], preferred_element_type=F32)
        rot[...] = (total * (1.0 / math.sqrt(HB * nt))).astype(BF16)
        copies = []
        for k in range(1, ndp):
            to = lax.rem(d + k, ndp)
            first = pl.multiple_of(window_start(z, to // 2) * tp, 16)
            copy = pltpu.make_async_remote_copy(
                src_ref=rot.at[pl.ds(first, nb * tp)], dst_ref=win.at[k], send_sem=win_s.at[k],
                recv_sem=win_r.at[k], device_id=(to, s), device_id_type=MESH)
            copy.start()
            copies.append(copy)
        return copies

    split = max(chips // 2, 1)
    for q in range(split):
        dequantize(q)
    wincopies = rotate()
    for q in range(split, chips):
        dequantize(q)

    mine = window_start(z, chip)
    first = pl.multiple_of(mine * tp, 16)
    win[0] = rot[pl.ds(first, nb * tp), :]
    for k in range(ndp):
        if k:
            wincopies[k - 1].wait_recv()
        for n in range(nb):
            wpad[k * tp:(k + 1) * tp, n * HB:(n + 1) * HB] = win[k, n * tp:(n + 1) * tp, :]
    t_id = lax.broadcasted_iota(I32, (tokens, ndp * tp), 0)
    q_id = lax.broadcasted_iota(I32, (tokens, ndp * tp), 1)
    slot = q_id // tp
    inner = q_id - slot * tp
    src = d - slot
    src = jnp.where(src < 0, src + ndp, src)
    pick = ((t_id == src * tl + inner) & (inner < tl)).astype(F32).astype(BF16)
    ordered = jnp.dot(pick, wpad[...], preferred_element_type=F32).astype(BF16)
    offset = chip * (2 * rows) - mine * HB
    f_id = lax.broadcasted_iota(I32, (nb * HB, rp), 0)
    r_id = lax.broadcasted_iota(I32, (nb * HB, rp), 1)
    for half in range(2):
        owner = lax.rem(core + half, 2)
        shift = ((f_id == offset + owner * rows + r_id) & (r_id < rows)).astype(F32).astype(BF16)
        lhs[half] = jnp.dot(ordered, shift, preferred_element_type=F32).astype(BF16)

    for copy in wcopies:
        copy.wait_recv()

    def product(k, kind, ch):
        span = slice(ch * cw, (ch + 1) * cw)
        return (jnp.dot(lhs[0], weights[0, k, kind, :, span], preferred_element_type=F32)
                + jnp.dot(lhs[1], wrecv[k, kind, :, span], preferred_element_type=F32))

    pcopies = {}
    for ch in range(nch):
        for k in range(1, chips):
            for kind in range(2):
                psend[k - 1, ch, kind] = product(k, kind, ch).astype(BF16)
            copy = pltpu.make_async_remote_copy(
                src_ref=psend.at[k - 1, ch], dst_ref=prec.at[k - 1, ch],
                send_sem=p_s.at[k - 1, ch], recv_sem=p_r.at[k - 1, ch],
                device_id=(lax.rem(chip + k, chips) * 2 + core, s), device_id_type=MESH)
            copy.start()
            pcopies[k, ch] = copy
        for kind in range(2):
            acc[ch, kind] = product(0, kind, ch)

    zcopies = {}
    for ch in range(nch):
        for k in range(1, chips):
            pcopies[k, ch].wait_recv()
        for kind in range(2):
            total = acc[ch, kind]
            for k in range(1, chips):
                total = total + prec[k - 1, ch, kind].astype(F32)
            acc[ch, kind] = total
        for k in range(1, nt):
            to = lax.rem(s + k, nt)
            part = pl.ds(pl.multiple_of(to * tt, 8), tt)
            zsend[k - 1, ch] = jnp.concatenate(
                [acc[ch, 0, part, :], acc[ch, 1, part, :]], axis=0).astype(BF16)
            copy = pltpu.make_async_remote_copy(
                src_ref=zsend.at[k - 1, ch], dst_ref=zrec.at[k - 1, ch],
                send_sem=z_s.at[k - 1, ch], recv_sem=z_r.at[k - 1, ch],
                device_id=(d, to), device_id_type=MESH)
            copy.start()
            zcopies[k, ch] = copy

    part = pl.ds(pl.multiple_of(s * tt, 8), tt)
    score = jnp.zeros((tt, 1), F32)
    for ch in range(nch):
        total = jnp.concatenate([acc[ch, 0, part, :], acc[ch, 1, part, :]], axis=0)
        for k in range(1, nt):
            zcopies[k, ch].wait_recv()
            total = total + zrec[k - 1, ch].astype(F32)
        out_ref[:, ch * cw:(ch + 1) * cw] = total[:tt].astype(BF16)
        gap = total[tt:]
        score = score + jnp.sum(gap * gap, axis=1, keepdims=True)
    srec[0] = jnp.broadcast_to(score / SCORE_DIVISOR, (tt, HB))
    scopies = []
    for k in range(1, ndp):
        copy = pltpu.make_async_remote_copy(
            src_ref=srec.at[0], dst_ref=srec.at[k], send_sem=s_s.at[k], recv_sem=s_r.at[k],
            device_id=(lax.rem(d + k, ndp), s), device_id_type=MESH)
        copy.start()
        scopies.append(copy)
    for copy in scopies:
        copy.wait_recv()
    total = jnp.zeros((tt, HB), F32)
    for j in range(ndp):
        total = total + srec[lax.rem(d - j + ndp, ndp)]
    score_ref[...] = total

    for copy in (xcopies + wincopies + wcopies + list(pcopies.values()) + list(zcopies.values())
                 + scopies):
        copy.wait_send()


def local(ndp, nt, activations, weight_codes, scale_index, scale_table, bit_widths):
    z = sizes(ndp, nt, activations.shape, weight_codes.shape)
    chips, cw, nch, tt, rp = z["chips"], z["cw"], z["nch"], z["tt"], z["rp"]
    tp, nb, nblk, cols, tokens = z["tp"], z["nb"], z["nblk"], z["cols"], z["tokens"]
    vmem = pl.BlockSpec(memory_space=pltpu.VMEM)
    dma = lambda *shape: pltpu.SemaphoreType.DMA(shape)
    others = max(chips - 1, 1)
    ties = max(nt - 1, 1)
    out, scores = pl.pallas_call(
        functools.partial(kernel, z),
        out_shape=(
            jax.ShapeDtypeStruct((tt, cols), BF16),
            jax.ShapeDtypeStruct((tt, HB), F32),
        ),
        in_specs=[vmem, pl.BlockSpec(memory_space=pl.ANY), vmem,
                  pl.BlockSpec(memory_space=pltpu.SMEM), vmem, vmem],
        out_specs=(vmem, vmem),
        scratch_shapes=[
            pltpu.VMEM(weight_codes.shape, I32),
            pltpu.VMEM((nt, nblk * tp, HB), BF16),
            pltpu.VMEM((nblk * tp, HB), BF16),
            pltpu.VMEM((ndp, nb * tp, HB), BF16),
            pltpu.VMEM((ndp * tp, nb * HB), BF16),
            pltpu.VMEM((2, tokens, rp), BF16),
            pltpu.VMEM((2, chips, 2, rp, cols), BF16),
            pltpu.VMEM((chips, 2, rp, cols), BF16),
            pltpu.VMEM((others, nch, 2, tokens, cw), BF16),
            pltpu.VMEM((others, nch, 2, tokens, cw), BF16),
            pltpu.VMEM((nch, 2, tokens, cw), F32),
            pltpu.VMEM((ties, nch, 2 * tt, cw), BF16),
            pltpu.VMEM((ties, nch, 2 * tt, cw), BF16),
            pltpu.VMEM((ndp, tt, HB), F32),
            dma(chips), dma(nt), dma(nt), dma(ndp), dma(ndp), dma(chips), dma(chips),
            dma(others, nch), dma(others, nch), dma(ties, nch), dma(ties, nch),
            dma(ndp), dma(ndp),
        ],
        compiler_params=pltpu.CompilerParams(
            collective_id=0, has_side_effects=True, vmem_limit_bytes=56 * 2 ** 20),
    )(activations, weight_codes, scale_index, scale_table, bit_widths[0],
      jnp.asarray(sylvester(HB), BF16))
    return out, scores[:, 0][None]


def solution(mesh):
    in_specs = (
        P("dp", "tensor"),
        P(("tensor", "dp"), None),
        P(("tensor", "dp"), None),
        P(),
        P(None, ("tensor", "dp"), None),
    )
    out_specs = (P("tensor", "dp"), P(None, "tensor"))
    body = functools.partial(local, mesh.shape["dp"], mesh.shape["tensor"])
    return jax.shard_map(body, mesh=mesh, in_specs=in_specs, out_specs=out_specs, check_vma=False)
```

time: 269 us -> 69.7 us (0.26)
  other arithmetic: 88.6 us -> 0 us
  local copies, waits for them, and re-layouts: 87.1 us -> 6.03 us
  Pallas kernels: 0 us -> 62.6 us
  waiting for transfers between devices: 30.7 us -> 0 us
  blocking collectives: 25.5 us -> 0 us
  starting transfers between devices: 16.9 us -> 0 us
  between operations: 14.1 us -> 0.64 us
  matrix products: 3.59 us -> 0 us
    convert_element_type x5 -> x0, other arithmetic: 80.6 us -> none  [the longest x1 72.8 us: dequantize(): ((grouped - 8).astype(jnp.float32) * scales[..., None]).astype(jnp.bfloat16)]
    pallas_call x0 -> x1, Pallas kernels: none -> 62.6 us  [local(): pl.pallas_call(functools.partial(kernel, z), out_shape=(jax.ShapeDtypeStr...]
    reduce_scatter x1 -> x0, waiting for transfers between devices: 28.8 us -> none  [local(): lax.psum_scatter(jnp.einsum('tf,kfd->tkd', all_tokens, local_weights, pre...]
    add x2 -> x0, local copies, waits for them, and re-layouts: 16.2 us -> none  [dequantize(): cand_codes = grouped[None] // step_size * step_size + step_size // 2]
    ne x2 -> x0, local copies, waits for them, and re-layouts: 16.1 us -> none  [dequantize(): cand_codes = grouped[None] // step_size * step_size + step_size // 2]
    rem x2 -> x0, local copies, waits for them, and re-layouts: 16.1 us -> none  [dequantize(): cand_codes = grouped[None] // step_size * step_size + step_size // 2]
    psum x1 -> x0, blocking collectives: 13.9 us -> none  [local(): scores = lax.psum(block_scores, 'dp')]
    convert_element_type x6 -> x0, local copies, waits for them, and re-layouts: 13.7 us -> none  [the longest x2 11.4 us: local(): local_grouped = code_home.astype(jnp.int32)]
  transfers between devices with their start and end apart: 6 -> 0, of which waited for: 2 -> 0; matrix products, arithmetic and copies ran while one was open for 33% -> 0% of each run, Pallas kernels for 0% -> 0%
where the time goes in v1:
time: 69.7 us; the launch traced here: 69.3 us
  Pallas kernels  62.6 us (90%)
  local copies, waits for them, and re-layouts  6.03 us (9%)
    pallas_call x1, Pallas kernels, local(): pl.pallas_call(functools.partial(kernel, z), out_shape=(jax.ShapeDtypeStr...  62.6 us
    unnamed x3, local copies, waits for them, and re-layouts  4.68 us

profile of v1, /device:TPU:0, one launch (start us, length us, event | category | flops | bytes accessed | tf_op | source)
XLA Modules:
  0.0 69.3 jit_solution(10547375156935990765)
XLA Ops:
  0.6 1.6 %copy.11.index_ref = s32[208,64]{1,0:T(8,128)} copy(s32[208,64]{0,1:T(8,128)} %param.8) | data formatting | bytes 106496 | tf_op args[2]
  2.2 1.6 %copy.10 = s32[1,208,64]{2,1,0:T(8,128)} copy(s32[1,208,64]{1,2,0:T(8,128)} %param.10) | data formatting | bytes 106496 | tf_op args[4]
  3.8 62.6 %shard_map.77 = (bf16[40,1024]{1,0:T(8,128)(2,1)}, f32[40,128]{1,0:T(8,128)}) custom-call(bf16[20,1664]{1,0:T(8,128)(2,1)} %act_ref.1, s32[208,8192]{1,0:T(8,128)} %code_hbm.1, s32[208,64]{1,0:T(8,128)} %copy.11.index_ref, f32[16]{0:T(128)} %table_ref.1, s32[208,64]{1,0:T(8,128)} %bitcast.2, bf16[128,128]{1,0:T(8,128)(2,1)} %constant.2.clone.had_ref), custom_call_target="tpu_custom_call" | custom-call | tf_op jit(solution)/shard_map/pallas_call | solution.py:256
  66.4 1.4 %slice_reduce_fusion = f32[40]{0:T(128)} fusion(f32[40,128]{1,0:T(8,128)} %get-tuple-element.5), kind=kLoop, calls=%fused_computation | loop fusion | bytes 320 | tf_op jit(solution)/shard_map/slice | solution.py:288
  67.8 1.5 %copy.13 = bf16[40,1024]{1,0:T(8,128)(2,1)} copy(bf16[40,1024]{1,0:T(8,128)(2,1)} %get-tuple-element.8) | data formatting | bytes 163840

commit v2 on v1

--- a/solution.py
+++ b/solution.py
@@ -30,7 +30,7 @@
 def sizes(ndp, nt, act_shape, code_shape):
     tl, width = act_shape
     rows, model = code_shape
-    z = dict(ndp=ndp, nt=nt, chips=ndp // 2, tl=tl, tp=up16(tl), nblk=width // HB, rows=rows)
+    z = dict(ndp=ndp, nt=nt, chips=ndp // 2, tl=tl, nblk=width // HB, rows=rows)
     z["rp"] = up16(rows)
     z["cols"] = model // ndp
     z["tokens"] = tl * ndp
@@ -40,30 +40,29 @@
     z["nb"] = min(max(spans), z["nblk"])
     z["cw"] = 256 if z["cols"] % 256 == 0 else z["cols"]
     z["nch"] = z["cols"] // z["cw"]
+    z["xr"] = up16(z["nblk"] * tl)
+    z["wr"] = up16(z["nb"] * tl)
+    z["starts"] = [min(c * pair // HB, z["nblk"] - z["nb"]) for c in range(z["chips"])]
     return z
 
 
-def window_start(z, chip):
-    return jnp.minimum(chip * (2 * z["rows"]) // HB, z["nblk"] - z["nb"])
-
-
 def kernel(z, act_ref, code_hbm, index_ref, table_ref, bits_ref, had_ref, out_ref, score_ref,
-           codes, xs, rot, win, wpad, lhs, weights, wrecv, psend, prec, acc, zsend, zrec, srec,
+           codes, xs, fat, wsend, win, wpad, shifts, lhs, weights, wrecv, psend, prec, acc, zsend, zrec, srec,
            code_sem, xs_s, xs_r, win_s, win_r, w_s, w_r, p_s, p_r, z_s, z_r, s_s, s_r):
     ndp, nt, chips = z["ndp"], z["nt"], z["chips"]
-    tl, tp, nblk, nb = z["tl"], z["tp"], z["nblk"], z["nb"]
+    tl, nblk, nb = z["tl"], z["nblk"], z["nb"]
     rows, rp, cols, tokens, tt = z["rows"], z["rp"], z["cols"], z["tokens"], z["tt"]
-    cw, nch = z["cw"], z["nch"]
+    cw, nch, xr, wr, starts = z["cw"], z["nch"], z["xr"], z["wr"], z["starts"]
     d = lax.axis_index("dp")
     s = lax.axis_index("tensor")
     chip, core = d // 2, d % 2
 
     loads = []
-    for q in range(chips):
-        span = pl.ds(q * 2 * cols, 2 * cols)
-        load = pltpu.make_async_copy(code_hbm.at[:, span], codes.at[:, span], code_sem.at[q])
-        load.start()
-        loads.append(load)
+    for k in range(chips):
+        span = pl.ds(pl.multiple_of(lax.rem(chip + k, chips) * (2 * cols), 128), 2 * cols)
+        loads.append(pltpu.make_async_copy(code_hbm.at[:, span], codes.at[k], code_sem.at[k]))
+    for k in [*range(1, chips), 0]:
+        loads[k].start()
 
     barrier = pltpu.get_barrier_semaphore()
     for k in range(1, ndp):
@@ -71,9 +70,11 @@
     for k in range(1, nt):
         pl.semaphore_signal(barrier, inc=1, device_id=(d, lax.rem(s + k, nt)), device_id_type=MESH)
 
-    xs[0] = jnp.zeros(xs.shape[1:], BF16)
+    act = act_ref[...].astype(F32)
+    fat[nblk * tl:, :] = jnp.zeros((xr + wr - nblk * tl, HB), F32)
     for n in range(nblk):
-        xs[0, n * tp:n * tp + tl, :] = act_ref[:, n * HB:(n + 1) * HB]
+        fat[n * tl:(n + 1) * tl, :] = act[:, n * HB:(n + 1) * HB]
+    xs[0] = fat[0:xr, :].astype(BF16)
 
     pl.semaphore_wait(barrier, ndp - 1 + nt - 1)
 
@@ -85,26 +86,44 @@
         copy.start()
         xcopies.append(copy)
 
+    f_id = lax.broadcasted_iota(I32, (nb * HB, rp), 0)
+    r_id = lax.broadcasted_iota(I32, (nb * HB, rp), 1)
+    mine = jnp.minimum(chip * (2 * rows) // HB, nblk - nb)
+    offset = chip * (2 * rows) - mine * HB
+    for half in range(2):
+        owner = lax.rem(core + half, 2)
+        shift = (f_id == offset + owner * rows + r_id) & (r_id < rows)
+        shifts[half] = shift.astype(F32).astype(BF16)
+
+    groups = cols // HB
+    lanes = index_ref.shape[0]
+
+    def columns(rowwise):
+        wide = jnp.concatenate([rowwise] * max(HB // lanes, 1), axis=0)
+        wide = jnp.transpose(wide)
+        turn = lax.rem(wide.shape[1] - lax.rem(chip * (2 * groups), wide.shape[1]), wide.shape[1])
+        return pltpu.roll(wide, turn, 1)
+
     index = index_ref[...]
     scales = jnp.zeros(index.shape, F32)
     for i in range(table_ref.shape[0]):
         scales = jnp.where(index == i, table_ref[i], scales)
     bits = bits_ref[...]
-    step = jnp.where(bits == 2, 4, jnp.where(bits == 3, 2, 1)).astype(I32)
+    scales = columns(scales)
+    step = columns(jnp.where(bits == 2, 4, jnp.where(bits == 3, 2, 1)).astype(I32))
 
     if rp != rows:
         weights[...] = jnp.zeros(weights.shape, BF16)
-    groups = cols // HB
-    wcopies = []
-
-    def dequantize(q):
-        rel = lax.rem(q - chip + chips, chips)
-        loads[q].wait()
+    wcopies = {}
+
+    def dequantize(rel):
+        loads[rel].wait()
         for half in range(2):
             away = lax.rem(core + half, 2)
             for g in range(groups):
-                gg = (q * 2 + half) * groups + g
-                c = codes[:, gg * HB:(gg + 1) * HB]
+                at = half * groups + g
+                gg = (rel * 2 * groups + at) % lanes
+                c = codes[rel, :, at * HB:(at + 1) * HB]
                 sc = scales[:, gg:gg + 1]
                 st = step[:, gg:gg + 1]
                 base = ((c - 8).astype(F32) * sc).astype(BF16)
@@ -113,13 +132,13 @@
                 weights[away, rel, 0, 0:rows, g * HB:(g + 1) * HB] = base
                 weights[away, rel, 1, 0:rows, g * HB:(g + 1) * HB] = gap
         copy = pltpu.make_async_remote_copy(
-            src_ref=weights.at[1, rel], dst_ref=wrecv.at[rel], send_sem=w_s.at[q],
-            recv_sem=w_r.at[q], device_id=(chip * 2 + 1 - core, s), device_id_type=MESH)
+            src_ref=weights.at[1, rel], dst_ref=wrecv.at[rel], send_sem=w_s.at[rel],
+            recv_sem=w_r.at[rel], device_id=(chip * 2 + 1 - core, s), device_id_type=MESH)
         copy.start()
-        wcopies.append(copy)
+        wcopies[rel] = copy
 
     def rotate():
-        total = jnp.zeros((nblk * tp, HB), F32)
+        total = jnp.zeros((xr, HB), F32)
         for k in range(nt):
             if k:
                 xcopies[k - 1].wait_recv()
@@ -129,68 +148,67 @@
                 parity = parity + (src // 2 ** b % 2) * (s // 2 ** b % 2)
             sign = (1 - 2 * (parity % 2)).astype(F32)
             total = total + sign * jnp.dot(xs[k], had_ref[...], preferred_element_type=F32)
-        rot[...] = (total * (1.0 / math.sqrt(HB * nt))).astype(BF16)
+        fat[0:xr, :] = total * (1.0 / math.sqrt(HB * nt))
+        for c in range(chips):
+            wsend[c] = fat[starts[c] * tl:starts[c] * tl + wr, :].astype(BF16)
         copies = []
         for k in range(1, ndp):
             to = lax.rem(d + k, ndp)
-            first = pl.multiple_of(window_start(z, to // 2) * tp, 16)
             copy = pltpu.make_async_remote_copy(
-                src_ref=rot.at[pl.ds(first, nb * tp)], dst_ref=win.at[k], send_sem=win_s.at[k],
+                src_ref=wsend.at[to // 2], dst_ref=win.at[d], send_sem=win_s.at[k],
                 recv_sem=win_r.at[k], device_id=(to, s), device_id_type=MESH)
             copy.start()
             copies.append(copy)
+        win[d] = wsend[chip]
         return copies
-
-    split = max(chips // 2, 1)
-    for q in range(split):
-        dequantize(q)
-    wincopies = rotate()
-    for q in range(split, chips):
-        dequantize(q)
-
-    mine = window_start(z, chip)
-    first = pl.multiple_of(mine * tp, 16)
-    win[0] = rot[pl.ds(first, nb * tp), :]
-    for k in range(ndp):
-        if k:
-            wincopies[k - 1].wait_recv()
-        for n in range(nb):
-            wpad[k * tp:(k + 1) * tp, n * HB:(n + 1) * HB] = win[k, n * tp:(n + 1) * tp, :]
-    t_id = lax.broadcasted_iota(I32, (tokens, ndp * tp), 0)
-    q_id = lax.broadcasted_iota(I32, (tokens, ndp * tp), 1)
-    slot = q_id // tp
-    inner = q_id - slot * tp
-    src = d - slot
-    src = jnp.where(src < 0, src + ndp, src)
-    pick = ((t_id == src * tl + inner) & (inner < tl)).astype(F32).astype(BF16)
-    ordered = jnp.dot(pick, wpad[...], preferred_element_type=F32).astype(BF16)
-    offset = chip * (2 * rows) - mine * HB
-    f_id = lax.broadcasted_iota(I32, (nb * HB, rp), 0)
-    r_id = lax.broadcasted_iota(I32, (nb * HB, rp), 1)
-    for half in range(2):
-        owner = lax.rem(core + half, 2)
-        shift = ((f_id == offset + owner * rows + r_id) & (r_id < rows)).astype(F32).astype(BF16)
-        lhs[half] = jnp.dot(ordered, shift, preferred_element_type=F32).astype(BF16)
-
-    for copy in wcopies:
-        copy.wait_recv()
 
     def product(k, kind, ch):
         span = slice(ch * cw, (ch + 1) * cw)
         return (jnp.dot(lhs[0], weights[0, k, kind, :, span], preferred_element_type=F32)
                 + jnp.dot(lhs[1], wrecv[k, kind, :, span], preferred_element_type=F32))
 
+    early = list(range(1, 1 + (chips - 1) // 3))
+    late = list(range(1 + (chips - 1) // 3, chips))
+    for k in early:
+        dequantize(k)
+    wincopies = rotate()
+    for k in late:
+        dequantize(k)
+
+    for copy in wincopies:
+        copy.wait_recv()
+    for j in range(ndp):
+        got = win[j].astype(F32)
+        for n in range(nb):
+            wpad[j * tl:(j + 1) * tl, n * HB:(n + 1) * HB] = got[n * tl:(n + 1) * tl, :]
+    ordered = wpad[...].astype(BF16)
+    for half in range(2):
+        lhs[half] = jnp.dot(ordered, shifts[half], preferred_element_type=F32).astype(BF16)
+
     pcopies = {}
+
+    def partial(k, ch):
+        for kind in range(2):
+            psend[k - 1, ch, kind] = product(k, kind, ch).astype(BF16)
+        copy = pltpu.make_async_remote_copy(
+            src_ref=psend.at[k - 1, ch], dst_ref=prec.at[k - 1, ch],
+            send_sem=p_s.at[k - 1, ch], recv_sem=p_r.at[k - 1, ch],
+            device_id=(lax.rem(chip + k, chips) * 2 + core, s), device_id_type=MESH)
+        copy.start()
+        pcopies[k, ch] = copy
+
+    for k in early:
+        wcopies[k].wait_recv()
+        for ch in range(nch):
+            partial(k, ch)
+    for k in late:
+        wcopies[k].wait_recv()
     for ch in range(nch):
-        for k in range(1, chips):
-            for kind in range(2):
-                psend[k - 1, ch, kind] = product(k, kind, ch).astype(BF16)
-            copy = pltpu.make_async_remote_copy(
-                src_ref=psend.at[k - 1, ch], dst_ref=prec.at[k - 1, ch],
-                send_sem=p_s.at[k - 1, ch], recv_sem=p_r.at[k - 1, ch],
-                device_id=(lax.rem(chip + k, chips) * 2 + core, s), device_id_type=MESH)
-            copy.start()
-            pcopies[k, ch] = copy
+        for k in late:
+            partial(k, ch)
+    dequantize(0)
+    wcopies[0].wait_recv()
+    for ch in range(nch):
         for kind in range(2):
             acc[ch, kind] = product(0, kind, ch)
 
@@ -240,7 +258,7 @@
         total = total + srec[lax.rem(d - j + ndp, ndp)]
     score_ref[...] = total
 
-    for copy in (xcopies + wincopies + wcopies + list(pcopies.values()) + list(zcopies.values())
+    for copy in (xcopies + wincopies + list(wcopies.values()) + list(pcopies.values()) + list(zcopies.values())
                  + scopies):
         copy.wait_send()
 
@@ -248,7 +266,7 @@
 def local(ndp, nt, activations, weight_codes, scale_index, scale_table, bit_widths):
     z = sizes(ndp, nt, activations.shape, weight_codes.shape)
     chips, cw, nch, tt, rp = z["chips"], z["cw"], z["nch"], z["tt"], z["rp"]
-    tp, nb, nblk, cols, tokens = z["tp"], z["nb"], z["nblk"], z["cols"], z["tokens"]
+    nb, cols, tokens = z["nb"], z["cols"], z["tokens"]
     vmem = pl.BlockSpec(memory_space=pltpu.VMEM)
     dma = lambda *shape: pltpu.SemaphoreType.DMA(shape)
     others = max(chips - 1, 1)
@@ -263,11 +281,13 @@
                   pl.BlockSpec(memory_space=pltpu.SMEM), vmem, vmem],
         out_specs=(vmem, vmem),
         scratch_shapes=[
-            pltpu.VMEM(weight_codes.shape, I32),
-            pltpu.VMEM((nt, nblk * tp, HB), BF16),
-            pltpu.VMEM((nblk * tp, HB), BF16),
-            pltpu.VMEM((ndp, nb * tp, HB), BF16),
-            pltpu.VMEM((ndp * tp, nb * HB), BF16),
+            pltpu.VMEM((chips, z["rows"], 2 * cols), I32),
+            pltpu.VMEM((nt, z["xr"], HB), BF16),
+            pltpu.VMEM((z["xr"] + z["wr"], HB), F32),
+            pltpu.VMEM((chips, z["wr"], HB), BF16),
+            pltpu.VMEM((ndp, z["wr"], HB), BF16),
+            pltpu.VMEM((tokens, nb * HB), F32),
+            pltpu.VMEM((2, nb * HB, rp), BF16),
             pltpu.VMEM((2, tokens, rp), BF16),
             pltpu.VMEM((2, chips, 2, rp, cols), BF16),
             pltpu.VMEM((chips, 2, rp, cols), BF16),
@@ -283,7 +303,7 @@
         ],
         compiler_params=pltpu.CompilerParams(
             collective_id=0, has_side_effects=True, vmem_limit_bytes=56 * 2 ** 20),
-    )(activations, weight_codes, scale_index, scale_table, bit_widths[0],
+    )(activations, weight_codes, scale_index.T, scale_table, bit_widths[0].T,
       jnp.asarray(sylvester(HB), BF16))
     return out, scores[:, 0][None]
 

time: 69.7 us -> 63 us (0.904)
  Pallas kernels: 62.6 us -> 59.3 us
  local copies, waits for them, and re-layouts: 6.03 us -> 2.88 us
    pallas_call x1, Pallas kernels: 62.6 us -> 59.3 us  [local(): pl.pallas_call(functools.partial(kernel, z), out_shape=(jax.ShapeDtypeStr...]
    unnamed x3 -> x1, local copies, waits for them, and re-layouts: 4.68 us -> 1.53 us
where the time goes in v2:
time: 63 us; the launch traced here: 62.8 us
  Pallas kernels  59.3 us (94%)
  local copies, waits for them, and re-layouts  2.88 us (5%)
  between operations  0.64 us (1%)
    pallas_call x1, Pallas kernels, local(): pl.pallas_call(functools.partial(kernel, z), out_shape=(jax.ShapeDtypeStr...  59.3 us
    unnamed x1, local copies, waits for them, and re-layouts  1.53 us
    slice x1, local copies, waits for them, and re-layouts, local(): return (out, scores[:, 0][None])  1.35 us

profile of v2, /device:TPU:0, one launch (start us, length us, event | category | flops | bytes accessed | tf_op | source)
XLA Modules:
  0.0 62.8 jit_solution(4128255587912450555)
XLA Ops:
  0.6 59.3 %shard_map.77 = (bf16[40,1024]{1,0:T(8,128)(2,1)}, f32[40,128]{1,0:T(8,128)}) custom-call(bf16[20,1664]{1,0:T(8,128)(2,1)} %act_ref.1, s32[208,8192]{1,0:T(8,128)} %code_hbm.1, s32[64,208]{1,0:T(8,128)} %bitcast.5, f32[16]{0:T(128)} %table_ref.1, s32[64,208]{1,0:T(8,128)} %bitcast.6, bf16[128,128]{1,0:T(8,128)(2,1)} %constant.2.clone.had_ref), custom_call_target="tpu_custom_call" | custom-call | tf_op jit(solution)/shard_map/pallas_call | solution.py:274
  59.9 1.4 %slice_reduce_fusion = f32[40]{0:T(128)} fusion(f32[40,128]{1,0:T(8,128)} %get-tuple-element.5), kind=kLoop, calls=%fused_computation | loop fusion | bytes 320 | tf_op jit(solution)/shard_map/slice | solution.py:308
  61.3 1.5 %copy.9 = bf16[40,1024]{1,0:T(8,128)(2,1)} copy(bf16[40,1024]{1,0:T(8,128)(2,1)} %get-tuple-element.8) | data formatting | bytes 163840

commit v3 on v2

--- a/solution.py
+++ b/solution.py
@@ -40,6 +40,7 @@
     z["nb"] = min(max(spans), z["nblk"])
     z["cw"] = 256 if z["cols"] % 256 == 0 else z["cols"]
     z["nch"] = z["cols"] // z["cw"]
+    z["tree"] = z["chips"] == 4 and z["tokens"] % 32 == 0
     z["xr"] = up16(z["nblk"] * tl)
     z["wr"] = up16(z["nb"] * tl)
     z["starts"] = [min(c * pair // HB, z["nblk"] - z["nb"]) for c in range(z["chips"])]
@@ -47,7 +48,7 @@
 
 
 def kernel(z, act_ref, code_hbm, index_ref, table_ref, bits_ref, had_ref, out_ref, score_ref,
-           codes, xs, fat, wsend, win, wpad, shifts, lhs, weights, wrecv, psend, prec, acc, zsend, zrec, srec,
+           codes, xs, fat, wsend, win, wpad, shifts, lhs, weights, wrecv, psend, prec, keep, acc, zsend, zrec, srec,
            code_sem, xs_s, xs_r, win_s, win_r, w_s, w_r, p_s, p_r, z_s, z_r, s_s, s_r):
     ndp, nt, chips = z["ndp"], z["nt"], z["chips"]
     tl, nblk, nb = z["tl"], z["nblk"], z["nb"]
@@ -169,6 +170,8 @@
 
     early = list(range(1, 1 + (chips - 1) // 3))
     late = list(range(1 + (chips - 1) // 3, chips))
+    if z["tree"]:
+        late = late[::-1]
     for k in early:
         dequantize(k)
     wincopies = rotate()
@@ -197,30 +200,82 @@
         copy.start()
         pcopies[k, ch] = copy
 
-    for k in early:
-        wcopies[k].wait_recv()
+    half_tokens = tokens // 2
+    odd = lax.rem(chip, 2)
+    near = (chip + 1 - 2 * odd, lax.rem(chip + 2, chips))
+    k_near = (1 + 2 * odd, 2)
+    k_far = 3 - 2 * odd
+
+    def ship(stage, h, ch, to):
+        at = stage * 2 + h
+        copy = pltpu.make_async_remote_copy(
+            src_ref=psend.at[at, ch], dst_ref=prec.at[at, ch], send_sem=p_s.at[at, ch],
+            recv_sem=p_r.at[at, ch], device_id=(to * 2 + core, s), device_id_type=MESH)
+        copy.start()
+        pcopies[at, ch] = copy
+
+    if z["tree"]:
+        wcopies[1].wait_recv()
+        wcopies[3].wait_recv()
         for ch in range(nch):
-            partial(k, ch)
-    for k in late:
-        wcopies[k].wait_recv()
-    for ch in range(nch):
+            for kind in range(2):
+                far = product(k_far, kind, ch).astype(BF16)
+                psend[0, ch, kind] = far[:half_tokens]
+                psend[1, ch, kind] = far[half_tokens:]
+            for h in range(2):
+                ship(0, h, ch, near[h])
+        dequantize(0)
+        wcopies[2].wait_recv()
+        wcopies[0].wait_recv()
+        for ch in range(nch):
+            for h in range(2):
+                for kind in range(2):
+                    block = product(k_near[h], kind, ch)
+                    first, second = block[:half_tokens], block[half_tokens:]
+                    psend[2 + h, ch, kind] = (second if h else first).astype(BF16)
+                    keep[1 - h, ch, kind] = first if h else second
+                ship(1, h, ch, near[h])
+            for h in range(2):
+                pcopies[h, ch].wait_recv()
+                for kind in range(2):
+                    psend[4 + h, ch, kind] = (
+                        keep[h, ch, kind] + prec[h, ch, kind].astype(F32)).astype(BF16)
+                ship(2, h, ch, near[1 - h])
+            for kind in range(2):
+                acc[ch, kind] = product(0, kind, ch)
+    else:
+        for k in early:
+            wcopies[k].wait_recv()
+            for ch in range(nch):
+                partial(k, ch)
         for k in late:
-            partial(k, ch)
-    dequantize(0)
-    wcopies[0].wait_recv()
-    for ch in range(nch):
-        for kind in range(2):
-            acc[ch, kind] = product(0, kind, ch)
+            wcopies[k].wait_recv()
+        for ch in range(nch):
+            for k in late:
+                partial(k, ch)
+        dequantize(0)
+        wcopies[0].wait_recv()
+        for ch in range(nch):
+            for kind in range(2):
+                acc[ch, kind] = product(0, kind, ch)
 
     zcopies = {}
     for ch in range(nch):
-        for k in range(1, chips):
-            pcopies[k, ch].wait_recv()
+        for (k, c), copy in pcopies.items():
+            if c == ch and not (z["tree"] and k < 2):
+                copy.wait_recv()
         for kind in range(2):
-            total = acc[ch, kind]
-            for k in range(1, chips):
-                total = total + prec[k - 1, ch, kind].astype(F32)
-            acc[ch, kind] = total
+            if z["tree"]:
+                for h in range(2):
+                    span = slice(h * half_tokens, (h + 1) * half_tokens)
+                    acc[ch, kind, span, :] = (acc[ch, kind, span, :]
+                                              + prec[2 + h, ch, kind].astype(F32)
+                                              + prec[4 + h, ch, kind].astype(F32))
+            else:
+                total = acc[ch, kind]
+                for k in range(1, chips):
+                    total = total + prec[k - 1, ch, kind].astype(F32)
+                acc[ch, kind] = total
         for k in range(1, nt):
             to = lax.rem(s + k, nt)
             part = pl.ds(pl.multiple_of(to * tt, 8), tt)
@@ -269,7 +324,7 @@
     nb, cols, tokens = z["nb"], z["cols"], z["tokens"]
     vmem = pl.BlockSpec(memory_space=pltpu.VMEM)
     dma = lambda *shape: pltpu.SemaphoreType.DMA(shape)
-    others = max(chips - 1, 1)
+    others, high = (6, tokens // 2) if z["tree"] else (max(chips - 1, 1), tokens)
     ties = max(nt - 1, 1)
     out, scores = pl.pallas_call(
         functools.partial(kernel, z),
@@ -291,8 +346,9 @@
             pltpu.VMEM((2, tokens, rp), BF16),
             pltpu.VMEM((2, chips, 2, rp, cols), BF16),
             pltpu.VMEM((chips, 2, rp, cols), BF16),
-            pltpu.VMEM((others, nch, 2, tokens, cw), BF16),
-            pltpu.VMEM((others, nch, 2, tokens, cw), BF16),
+            pltpu.VMEM((others, nch, 2, high, cw), BF16),
+            pltpu.VMEM((others, nch, 2, high, cw), BF16),
+            pltpu.VMEM((2, nch, 2, high, cw) if z["tree"] else (8, HB), F32),
             pltpu.VMEM((nch, 2, tokens, cw), F32),
             pltpu.VMEM((ties, nch, 2 * tt, cw), BF16),
             pltpu.VMEM((ties, nch, 2 * tt, cw), BF16),

time: 63 us -> 55.3 us (0.88)
  Pallas kernels: 59.3 us -> 51.5 us
    pallas_call x1, Pallas kernels: 59.3 us -> 51.5 us  [local(): pl.pallas_call(functools.partial(kernel, z), out_shape=(jax.ShapeDtypeStr...]
where the time goes in v3:
time: 55.3 us; the launch traced here: 55 us
  Pallas kernels  51.5 us (93%)
  local copies, waits for them, and re-layouts  2.88 us (5%)
  between operations  0.64 us (1%)
    pallas_call x1, Pallas kernels, local(): pl.pallas_call(functools.partial(kernel, z), out_shape=(jax.ShapeDtypeStr...  51.5 us
    unnamed x1, local copies, waits for them, and re-layouts  1.53 us
    slice x1, local copies, waits for them, and re-layouts, local(): return (out, scores[:, 0][None])  1.35 us

profile of v3, /device:TPU:0, one launch (start us, length us, event | category | flops | bytes accessed | tf_op | source)
XLA Modules:
  0.0 55.0 jit_solution(13205080238842213547)
XLA Ops:
  0.6 51.5 %shard_map.77 = (bf16[40,1024]{1,0:T(8,128)(2,1)}, f32[40,128]{1,0:T(8,128)}) custom-call(bf16[20,1664]{1,0:T(8,128)(2,1)} %act_ref.1, s32[208,8192]{1,0:T(8,128)} %code_hbm.1, s32[64,208]{1,0:T(8,128)} %bitcast.5, f32[16]{0:T(128)} %table_ref.1, s32[64,208]{1,0:T(8,128)} %bitcast.6, bf16[128,128]{1,0:T(8,128)(2,1)} %constant.2.clone.had_ref), custom_call_target="tpu_custom_call" | custom-call | tf_op jit(solution)/shard_map/pallas_call | solution.py:329
  52.2 1.4 %slice_reduce_fusion = f32[40]{0:T(128)} fusion(f32[40,128]{1,0:T(8,128)} %get-tuple-element.5), kind=kLoop, calls=%fused_computation | loop fusion | bytes 320 | tf_op jit(solution)/shard_map/slice | solution.py:364
  53.5 1.5 %copy.9 = bf16[40,1024]{1,0:T(8,128)(2,1)} copy(bf16[40,1024]{1,0:T(8,128)(2,1)} %get-tuple-element.8) | data formatting | bytes 163840

commit v4 on v3

--- a/solution.py
+++ b/solution.py
@@ -171,7 +171,7 @@
     early = list(range(1, 1 + (chips - 1) // 3))
     late = list(range(1 + (chips - 1) // 3, chips))
     if z["tree"]:
-        late = late[::-1]
+        late = [3]
     for k in early:
         dequantize(k)
     wincopies = rotate()
@@ -224,6 +224,7 @@
                 psend[1, ch, kind] = far[half_tokens:]
             for h in range(2):
                 ship(0, h, ch, near[h])
+        dequantize(2)
         dequantize(0)
         wcopies[2].wait_recv()
         wcopies[0].wait_recv()

time: 55.3 us -> 55.3 us (level)
  no operation moved by 1% of the time
where the time goes in v4:
time: 55.3 us; the launch traced here: 55 us
  Pallas kernels  51.5 us (93%)
  local copies, waits for them, and re-layouts  2.88 us (5%)
  between operations  0.64 us (1%)
    pallas_call x1, Pallas kernels, local(): pl.pallas_call(functools.partial(kernel, z), out_shape=(jax.ShapeDtypeStr...  51.5 us
    unnamed x1, local copies, waits for them, and re-layouts  1.53 us
    slice x1, local copies, waits for them, and re-layouts, local(): return (out, scores[:, 0][None])  1.35 us

profile of v4, /device:TPU:0, one launch (start us, length us, event | category | flops | bytes accessed | tf_op | source)
XLA Modules:
  0.0 55.0 jit_solution(10713011344966270669)
XLA Ops:
  0.6 51.5 %shard_map.77 = (bf16[40,1024]{1,0:T(8,128)(2,1)}, f32[40,128]{1,0:T(8,128)}) custom-call(bf16[20,1664]{1,0:T(8,128)(2,1)} %act_ref.1, s32[208,8192]{1,0:T(8,128)} %code_hbm.1, s32[64,208]{1,0:T(8,128)} %bitcast.5, f32[16]{0:T(128)} %table_ref.1, s32[64,208]{1,0:T(8,128)} %bitcast.6, bf16[128,128]{1,0:T(8,128)(2,1)} %constant.2.clone.had_ref), custom_call_target="tpu_custom_call" | custom-call | tf_op jit(solution)/shard_map/pallas_call | solution.py:330
  52.2 1.4 %slice_reduce_fusion = f32[40]{0:T(128)} fusion(f32[40,128]{1,0:T(8,128)} %get-tuple-element.5), kind=kLoop, calls=%fused_computation | loop fusion | bytes 320 | tf_op jit(solution)/shard_map/slice | solution.py:365
  53.5 1.5 %copy.9 = bf16[40,1024]{1,0:T(8,128)(2,1)} copy(bf16[40,1024]{1,0:T(8,128)(2,1)} %get-tuple-element.8) | data formatting | bytes 163840
